TPU v7x, 256 devices: a whole 4x4x8 slice. The times are simulated.
256 devices in a mesh: batch: 64 (over y, x, z_hi), chan: 4 (over z_lo, core).
Axes of the slice: x: 4, y: 4, z: 8 (z_hi: 4, z_lo: 2; z = z_hi * 2 + z_lo), core: 2. Of those that a mesh axis runs over, the one named last changes fastest.
Arguments:
- fine_inputs: bfloat16 [64, 32, 32, 512], P('batch'), may hold values from -6 to 6
- fine_upstream: bfloat16 [64, 32, 32, 512], P('batch', None, None, 'chan'), may hold values from -6 to 6
- fine_bank: bfloat16 [8, 9, 512, 512], P(None, None, 'batch', 'chan'), may hold values from -0.09375 to 0.09375
- fine_coefs: float32 [64, 8], replicated, may hold values from 0 to 1, as said below
- coarse_inputs: bfloat16 [64, 16, 16, 512], P('batch'), may hold values from -6 to 6
- coarse_upstream: bfloat16 [64, 16, 16, 512], P('batch', None, None, 'chan'), may hold values from -6 to 6
- coarse_bank: bfloat16 [8, 9, 512, 512], P(None, None, 'batch', 'chan'), may hold values from -0.09375 to 0.09375
- coarse_coefs: float32 [64, 8], replicated, may hold values from 0 to 1, as said below
Outputs:
- fine_delta: bfloat16 [64, 32, 32, 512], P('batch', None, None, 'chan')
- fine_update: float32 [8, 9, 512, 512], P(None, None, 'batch', 'chan')
- fine_logit: float32 [64, 8], P('batch')
- coarse_delta: bfloat16 [64, 16, 16, 512], P('batch', None, None, 'chan')
- coarse_update: float32 [8, 9, 512, 512], P(None, None, 'batch', 'chan')
- coarse_logit: float32 [64, 8], P('batch')
Inputs may be any that keep to these rules, and one draw needn't show every extreme that they name: Each row of fine_coefs is a softmax: positive entries that sum to one. Each row of coarse_coefs is a softmax: positive entries that sum to one.
All inputs are finite; a program needn't handle non-finite values.
Results may differ from a plain program's by a relative error of at most 0.01.
Values may be sent and summed in bfloat16 or wider, within the bound.
A program may use at most 128 MiB of HBM per device.

v0:
```python
import jax
import jax.numpy as jnp
from jax import lax
from jax.sharding import PartitionSpec as P

BANKS = 8
FINE_SIDE = 32
COARSE_SIDE = 16
HIGH = lax.Precision.HIGHEST


def shifted(padded, row_shift, col_shift, side):
    window = padded[:, row_shift : row_shift + side, col_shift : col_shift + side, :]
    return window.reshape(window.shape[0], side * side, window.shape[3])


def local_grads(inputs, upstream, kernels, side):
    samples_here = inputs.shape[0]
    pad_in = jnp.pad(inputs, ((0, 0), (1, 1), (1, 1), (0, 0)))
    pad_up = jnp.pad(upstream, ((0, 0), (1, 1), (1, 1), (0, 0)))
    flat_up = upstream.reshape(samples_here, side * side, upstream.shape[3])
    delta = jnp.zeros((samples_here, side * side, inputs.shape[3]), jnp.float32)
    grad_taps = []
    for row_shift in range(3):
        for col_shift in range(3):
            tap = 3 * row_shift + col_shift
            window_in = shifted(pad_in, row_shift, col_shift, side)
            window_up = shifted(pad_up, 2 - row_shift, 2 - col_shift, side)
            grad_taps.append(
                jnp.einsum("bpc,bpo->bco", window_in, flat_up, preferred_element_type=jnp.float32)
                / side
            )
            delta = delta + jnp.einsum(
                "bpo,bco->bpc", window_up, kernels[:, tap], preferred_element_type=jnp.float32
            )
    return (delta.reshape(samples_here, side, side, inputs.shape[3]), jnp.stack(grad_taps, axis=1))


def one_layer(inputs, upstream, bank_part, coefs, side):
    samples_here = inputs.shape[0]
    first_row = lax.axis_index("batch") * samples_here
    own_coefs = lax.dynamic_slice_in_dim(coefs, first_row, samples_here, 0)
    flat_bank = bank_part.reshape(BANKS, -1).astype(jnp.float32)
    bank_rows = lax.all_gather(bank_part, "batch", axis=2, tiled=True)
    flat_rows = bank_rows.reshape(bank_rows.shape[0], -1).astype(jnp.float32)
    mixed = jnp.dot(own_coefs, flat_rows, precision=HIGH)
    kernels = mixed.reshape((samples_here,) + bank_rows.shape[1:]).astype(jnp.bfloat16)
    delta, kernel_grad = local_grads(inputs, upstream, kernels, side)
    delta_total = lax.psum(delta.astype(jnp.bfloat16), "chan").astype(jnp.float32)
    width = delta.shape[3] // lax.axis_size("chan")
    delta_part = lax.dynamic_slice_in_dim(delta_total, lax.axis_index("chan") * width, width, 3)
    moved = lax.all_to_all(
        kernel_grad.astype(jnp.bfloat16), "batch", split_axis=2, concat_axis=0, tiled=True
    ).astype(kernel_grad.dtype)
    flat_grads = moved.reshape(moved.shape[0], -1)
    update = jnp.dot(coefs.T, flat_grads, precision=HIGH).reshape(bank_part.shape)
    dcoef_part = lax.dot_general(flat_grads, flat_bank, (((1,), (1,)), ((), ())), precision=HIGH)
    return (delta_part.astype(jnp.bfloat16), update, dcoef_part)


def logit_grads(coefs, totals, samples_here):
    first_row = lax.axis_index("batch") * samples_here
    own_coefs = lax.dynamic_slice_in_dim(coefs, first_row, samples_here, 0)
    own_totals = lax.dynamic_slice_in_dim(totals, first_row, samples_here, 0)
    return own_coefs * (own_totals - jnp.sum(own_coefs * own_totals, axis=1, keepdims=True))


def per_device(
    fine_inputs,
    fine_upstream,
    fine_bank,
    fine_coefs,
    coarse_inputs,
    coarse_upstream,
    coarse_bank,
    coarse_coefs,
):
    fine_delta, fine_update, fine_partial = one_layer(
        fine_inputs, fine_upstream, fine_bank, fine_coefs, FINE_SIDE
    )
    coarse_delta, coarse_update, coarse_partial = one_layer(
        coarse_inputs, coarse_upstream, coarse_bank, coarse_coefs, COARSE_SIDE
    )
    fine_total, coarse_total = lax.psum((fine_partial, coarse_partial), ("batch", "chan"))
    samples_here = fine_inputs.shape[0]
    fine_logit = logit_grads(fine_coefs, fine_total, samples_here)
    coarse_logit = logit_grads(coarse_coefs, coarse_total, samples_here)
    return (fine_delta, fine_update, fine_logit, coarse_delta, coarse_update, coarse_logit)


def solution(mesh):
    return jax.shard_map(
        per_device,
        mesh=mesh,
        in_specs=(
            P("batch", None, None, None),
            P("batch", None, None, "chan"),
            P(None, None, "batch", "chan"),
            P(),
            P("batch", None, None, None),
            P("batch", None, None, "chan"),
            P(None, None, "batch", "chan"),
            P(),
        ),
        out_specs=(
            P("batch", None, None, "chan"),
            P(None, None, "batch", "chan"),
            P("batch", None),
            P("batch", None, None, "chan"),
            P(None, None, "batch", "chan"),
            P("batch", None),
        ),
        check_vma=False,
    )
```

profile of v0, /device:TPU:1, one launch (start us, length us, event | category | flops | bytes accessed | tf_op | source)
XLA Modules:
  0.0 524.2 jit_solution(8585332356747162847)
XLA Ops:
  7.2 0.7 all-gather.5.cloned.1.call-update
  8.0 0.7 all-gather.3.cloned.1.call-update
  8.7 1.2 fusion.60
  12.3 2.2 copy.31
  14.5 15.2 %all-to-all-start.1 = ((bf16[1,9,512,128]{3,1,0,2:T(8,128)(2,1)}), bf16[1,9,512,128]{3,1,0,2:T(8,128)(2,1)S(1)}, u32[]{:S(2)}, u32[]{:S(2)}) async-start(bf16[1,9,512,128]{3,1,0,2:T(8,128)(2,1)} %copy.31), calls=%async_computation.1 | async-start | bytes 4194304 | tf_op jit(solution)/shard_map/all_to_all | solution.py:52
  30.3 0.5 fusion.76
  30.8 0.5 fusion.74
  31.4 0.5 fusion.72
  31.9 0.5 fusion.70
  32.5 0.5 fusion.68
  33.0 0.6 fusion.66
  33.6 0.5 fusion.64
  34.1 0.5 fusion.62
  34.7 2.2 copy.28
  36.9 51.0 %all-to-all-done.1 = bf16[1,9,512,128]{3,1,0,2:T(8,128)(2,1)S(1)} async-done(((bf16[1,9,512,128]{3,1,0,2:T(8,128)(2,1)}), bf16[1,9,512,128]{3,1,0,2:T(8,128)(2,1)S(1)}, u32[]{:S(2)}, u32[]{:S(2)}) %all-to-all-start.1) | async-done | bytes 1179680 | tf_op jit(solution)/shard_map/all_to_all | solution.py:52
  87.9 5.9 %all-to-all-start = ((bf16[1,9,512,128]{3,1,0,2:T(8,128)(2,1)}), bf16[1,9,512,128]{3,1,0,2:T(8,128)(2,1)}, u32[]{:S(2)}, u32[]{:S(2)}) async-start(bf16[1,9,512,128]{3,1,0,2:T(8,128)(2,1)} %copy.28), calls=%async_computation | async-start | bytes 4194304 | tf_op jit(solution)/shard_map/all_to_all | solution.py:52
  94.1 0.6 copy.41
  94.7 0.6 copy.40
  95.3 0.8 pad_slice_fusion.24
  96.1 1.3 pad_slice_fusion.16
  97.8 1.3 reshape.891
  99.1 48.8 %all-to-all-done = bf16[1,9,512,128]{3,1,0,2:T(8,128)(2,1)} async-done(((bf16[1,9,512,128]{3,1,0,2:T(8,128)(2,1)}), bf16[1,9,512,128]{3,1,0,2:T(8,128)(2,1)}, u32[]{:S(2)}, u32[]{:S(2)}) %all-to-all-start) | async-done | bytes 1179680 | tf_op jit(solution)/shard_map/all_to_all | solution.py:52
  148.0 2.0 copy.61
  150.0 0.5 reshape.858
  150.5 0.6 fusion.166
  151.1 80.3 %all-gather.5.cloned.1.call-done = bf16[8,9,512,128]{3,2,1,0:T(8,128)(2,1)} async-done(((bf16[8,9,8,128]{3,2,1,0:T(8,128)(2,1)}), bf16[8,9,512,128]{3,2,1,0:T(8,128)(2,1)}) %all-gather.5.cloned.1.call-update) | async-done | bytes 9437200 | tf_op jit(solution)/shard_map/all_gather | solution.py:44
  231.4 16.2 %copy.58 = bf16[1,8,4608,128]{3,1,2,0:T(8,128)(2,1)S(1)} copy(bf16[1,8,4608,128]{3,2,1,0:T(8,128)(2,1)} %bitcast.537) | data formatting | bytes 18874368
  247.6 8.0 %fusion.146 = f32[1,9,512,128]{3,0,2,1:T(1,128)S(1)} fusion(bf16[9,512,128,8]{2,3,1,0:T(8,128)(2,1)S(1)} %bitcast.532, f32[1,8]{0,1:T(8,128)S(1)} %get-tuple-element.44), kind=kOutput, calls=%fused_computation.215 | convolution fusion | flops 56623104 | bytes 11796512 | tf_op jit(solution)/shard_map/dot_general | solution.py:46
  255.8 136.1 %all-gather.3.cloned.1.call-done = bf16[8,9,512,128]{3,2,1,0:T(8,128)(2,1)} async-done(((bf16[8,9,8,128]{3,2,1,0:T(8,128)(2,1)}), bf16[8,9,512,128]{3,2,1,0:T(8,128)(2,1)}) %all-gather.3.cloned.1.call-update) | async-done | bytes 9437200 | tf_op jit(solution)/shard_map/all_gather | solution.py:44
  391.9 16.2 %copy.59 = bf16[1,8,4608,128]{3,1,2,0:T(8,128)(2,1)S(1)} copy(bf16[1,8,4608,128]{3,2,1,0:T(8,128)(2,1)} %bitcast.536) | data formatting | bytes 18874368
  408.1 8.3 %fusion.148 = f32[1,9,512,128]{3,0,2,1:T(1,128)S(1)} fusion(bf16[9,512,128,8]{2,3,1,0:T(8,128)(2,1)S(1)} %bitcast.533, f32[1,8]{0,1:T(8,128)S(1)} %get-tuple-element.45), kind=kOutput, calls=%fused_computation.217 | convolution fusion | flops 56623104 | bytes 11796512 | tf_op jit(solution)/shard_map/dot_general | solution.py:46
  416.6 0.8 copy-done.9
  417.8 0.5 copy-done.8
  418.7 0.5 copy-done.7
  419.7 0.5 copy-done.6
  427.9 0.9 fusion.6
  428.8 1.9 fusion.4
  430.7 1.2 copy-done
  432.0 0.6 fusion.167
  432.5 0.8 copy.33
  433.3 0.8 copy.34
  435.0 76.0 %all-reduce.4 = (f32[64,8]{1,0:T(8,128)S(1)}, f32[64,8]{1,0:T(8,128)S(1)}) all-reduce(f32[64,8]{1,0:T(8,128)S(1)} %fusion.125, f32[64,8]{1,0:T(8,128)S(1)} %fusion.122), channel_id=1, replica_groups=mesh['batch'=64,'chan'=4] {'batch','chan'}, use_global_device_ids=true, to_apply=%region_1.2 | all-reduce | flops 1024 | bytes 8192 | tf_op jit(solution)/shard_map/psum | solution.py:84
  511.0 0.6 multiply_reduce_fusion
  511.6 0.6 multiply_reduce_fusion.1
  512.2 1.2 subtract_multiply_fusion
  513.3 1.2 subtract_multiply_fusion.1
  514.5 1.7 convert_convert_fusion
  516.2 1.5 convert_convert_fusion.1
  (87 shorter events, 13.6 us)
Async XLA Ops:
  7.2 2.8 copy-start.10
  7.2 2.7 copy-start.27
  7.2 224.2 %all-gather.5.cloned.1.call-start = ((), (), s32[]{:S(2)}) async-start(), calls=%async_computation.3 | async-start | bytes 9584640 | tf_op jit(solution)/shard_map/all_gather | solution.py:44
  7.9 384.0 %all-gather.3.cloned.1.call-start = ((), (), s32[]{:S(2)}) async-start(), calls=%async_computation.2 | async-start | bytes 9584640 | tf_op jit(solution)/shard_map/all_gather | solution.py:44
  14.5 15.3 %copy-start.1 = (bf16[1,32,32,128]{3,2,1,0:T(8,128)(2,1)S(1)}, bf16[1,32,32,128]{3,2,1,0:T(8,128)(2,1)}, u32[]{:S(2)}) copy-start(bf16[1,32,32,128]{3,2,1,0:T(8,128)(2,1)} %param.9) | copy-start | bytes 786436
  14.5 15.3 %copy-start.26 = (bf16[1,32,32,512]{3,2,1,0:T(8,128)(2,1)S(1)}, bf16[1,32,32,512]{3,2,1,0:T(8,128)(2,1)}, u32[]{:S(2)}) copy-start(bf16[1,32,32,512]{3,2,1,0:T(8,128)(2,1)} %param.8) | copy-start | bytes 3145732
  14.5 73.4 %all-to-all-start.1 = ((bf16[1,9,512,128]{3,1,0,2:T(8,128)(2,1)}), bf16[1,9,512,128]{3,1,0,2:T(8,128)(2,1)S(1)}, u32[]{:S(2)}, u32[]{:S(2)}) async-start(bf16[1,9,512,128]{3,1,0,2:T(8,128)(2,1)} %copy.31), calls=%async_computation.1 | async-start | bytes 4194304 | tf_op jit(solution)/shard_map/all_to_all | solution.py:52
  36.9 57.2 %copy-start.22 = (f32[64,8]{0,1:T(8,128)S(1)}, f32[64,8]{0,1:T(8,128)}, u32[]{:S(2)}) copy-start(f32[64,8]{0,1:T(8,128)} %param.11) | copy-start | bytes 6148
  36.9 57.2 %copy-start.23 = (f32[64,8]{0,1:T(8,128)S(1)}, f32[64,8]{0,1:T(8,128)}, u32[]{:S(2)}) copy-start(f32[64,8]{0,1:T(8,128)} %param.15) | copy-start | bytes 6148
  87.9 60.1 %all-to-all-start = ((bf16[1,9,512,128]{3,1,0,2:T(8,128)(2,1)}), bf16[1,9,512,128]{3,1,0,2:T(8,128)(2,1)}, u32[]{:S(2)}, u32[]{:S(2)}) async-start(bf16[1,9,512,128]{3,1,0,2:T(8,128)(2,1)} %copy.28), calls=%async_computation | async-start | bytes 4194304 | tf_op jit(solution)/shard_map/all_to_all | solution.py:52
  93.8 420.7 %all-reduce.8.cloned.1.call-start = ((), (), s32[]{:S(2)}) async-start(), calls=%async_computation.4 | async-start | bytes 2621440 | tf_op jit(solution)/shard_map/psum | solution.py:49
  416.4 1.0 copy-start.9
  417.3 0.9 copy-start.8
  418.3 0.9 copy-start.7
  419.2 0.9 copy-start.6
  420.2 0.9 copy-start.5
  421.1 0.9 copy-start.4
  422.1 0.9 copy-start.3
  423.0 0.9 copy-start.2
  424.0 0.8 copy-start.18
  424.0 1.1 copy-start.17
  424.4 0.9 copy-start.16
  425.1 0.8 copy-start.15
  425.3 0.8 copy-start.11
  425.9 0.8 copy-start.14
  426.2 0.8 copy-start.13
  426.8 0.8 copy-start.12
  427.0 0.8 copy-start.19
  430.7 1.3 copy-start
  431.9 2.1 copy-start.20
  433.3 1.2 copy-start.21
  434.5 76.4 %copy-start.25 = (f32[1,8]{1,0:T(1,128)S(1)}, f32[1,8]{1,0:T(1,128)}, u32[]{:S(2)}) copy-start(f32[1,8]{1,0:T(1,128)} %copy.41) | copy-start | bytes 100
  434.5 77.0 %copy-start.24 = (f32[1,8]{1,0:T(1,128)S(1)}, f32[1,8]{1,0:T(1,128)}, u32[]{:S(2)}) copy-start(f32[1,8]{1,0:T(1,128)} %copy.40) | copy-start | bytes 100
Sparse Core Ops, SparseCore 0:
  11.1 220.1 all-gather.4
  234.5 157.3 all-gather.2
  430.8 49.6 all-reduce.7
where the time goes:
time: 525 us; the launch traced here: 524 us
  waiting for transfers between devices  318 us (61%)
  blocking collectives  76 us (14%)
  local copies, waits for them, and re-layouts  53.3 us (10%)
  matrix products  34.7 us (7%)
  starting transfers between devices  21.4 us (4%)
  between operations  14.2 us (3%)
  other arithmetic  7.02 us (1%)
    all_gather x2, waiting for transfers between devices, one_layer(): bank_rows = lax.all_gather(bank_part, 'batch', axis=2, tiled=True)  216 us
    all_to_all x2, waiting for transfers between devices, one_layer(): lax.all_to_all(kernel_grad.astype(jnp.bfloat16), 'batch', split_axis=2, c...  99.9 us
    psum x1, blocking collectives, per_device(): lax.psum((fine_partial, coarse_partial), ('batch', 'chan'))  76 us
    unnamed x62, local copies, waits for them, and re-layouts  42.3 us
    all_to_all x2, starting transfers between devices, one_layer(): lax.all_to_all(kernel_grad.astype(jnp.bfloat16), 'batch', split_axis=2, c...  21.1 us
    dot_general x2, matrix products, one_layer(): mixed = jnp.dot(own_coefs, flat_rows, precision=HIGH)  16.3 us
  transfers between devices with their start and end apart: 5, of which 4 were waited for; matrix products, arithmetic and copies ran while one was open for 10% of the time, Pallas kernels for 0%

commit v1 on v0

--- a/solution.py
+++ b/solution.py
@@ -41,7 +41,9 @@
     first_row = lax.axis_index("batch") * samples_here
     own_coefs = lax.dynamic_slice_in_dim(coefs, first_row, samples_here, 0)
     flat_bank = bank_part.reshape(BANKS, -1).astype(jnp.float32)
-    bank_rows = lax.all_gather(bank_part, "batch", axis=2, tiled=True)
+    bank_rows = jnp.concatenate(
+        lax.all_to_all(jnp.stack([bank_part] * lax.axis_size("batch")), "batch", 0, 0), axis=2
+    )
     flat_rows = bank_rows.reshape(bank_rows.shape[0], -1).astype(jnp.float32)
     mixed = jnp.dot(own_coefs, flat_rows, precision=HIGH)
     kernels = mixed.reshape((samples_here,) + bank_rows.shape[1:]).astype(jnp.bfloat16)

time: 525 us -> 838 us (1.60); the launches traced: 524 us -> 828 us
  blocking collectives: 76 us -> 468 us
  waiting for transfers between devices: 318 us -> 202 us
  local copies, waits for them, and re-layouts: 53.3 us -> 80.6 us
    all_gather x2 -> x0, waiting for transfers between devices: 216 us -> none  [one_layer(): bank_rows = lax.all_gather(bank_part, 'batch', axis=2, tiled=True)]
    all_to_all x0 -> x2, blocking collectives: none -> 214 us  [the longest x1 168 us: one_layer(): lax.all_to_all(jnp.stack([bank_part] * lax.axis_size('batch')), 'batch',...]
    psum x1, blocking collectives: 76 us -> 254 us  [per_device(): lax.psum((fine_partial, coarse_partial), ('batch', 'chan'))]
    all_to_all x0 -> x1, waiting for transfers between devices: none -> 158 us  [one_layer(): lax.all_to_all(jnp.stack([bank_part] * lax.axis_size('batch')), 'batch',...]
    all_to_all x2 -> x1, waiting for transfers between devices: 99.9 us -> 44.3 us  [one_layer(): lax.all_to_all(kernel_grad.astype(jnp.bfloat16), 'batch', split_axis=2, c...]
    reshape x0 -> x2, local copies, waits for them, and re-layouts: none -> 20.1 us  [one_layer(): jnp.concatenate(lax.all_to_all(jnp.stack([bank_part] * lax.axis_size('bat...]
    all_to_all x2 -> x1, starting transfers between devices: 21.1 us -> 15.2 us  [one_layer(): lax.all_to_all(kernel_grad.astype(jnp.bfloat16), 'batch', split_axis=2, c...]
    unnamed x62 -> x72, local copies, waits for them, and re-layouts: 42.3 us -> 43.2 us
  transfers between devices with their start and end apart: 5 -> 3, of which waited for: 4 -> 2; matrix products, arithmetic and copies ran while one was open for 10% -> 7% of each run, Pallas kernels for 0% -> 0%
where the time goes in v1:
time: 838 us; the launch traced here: 828 us
  blocking collectives  468 us (56%)
  waiting for transfers between devices  202 us (24%)
  local copies, waits for them, and re-layouts  80.6 us (10%)
  matrix products  34.6 us (4%)
  starting transfers between devices  21.2 us (3%)
  between operations  14.9 us (2%)
    psum x1, blocking collectives, per_device(): lax.psum((fine_partial, coarse_partial), ('batch', 'chan'))  254 us
    all_to_all x1, blocking collectives, one_layer(): lax.all_to_all(jnp.stack([bank_part] * lax.axis_size('batch')), 'batch',...  168 us
    all_to_all x1, waiting for transfers between devices, one_layer(): lax.all_to_all(jnp.stack([bank_part] * lax.axis_size('batch')), 'batch',...  158 us
    all_to_all x1, blocking collectives, one_layer(): lax.all_to_all(kernel_grad.astype(jnp.bfloat16), 'batch', split_axis=2, c...  45.8 us
    all_to_all x1, waiting for transfers between devices, one_layer(): lax.all_to_all(kernel_grad.astype(jnp.bfloat16), 'batch', split_axis=2, c...  44.3 us
    unnamed x72, local copies, waits for them, and re-layouts  43.2 us
    reshape x2, local copies, waits for them, and re-layouts, one_layer(): jnp.concatenate(lax.all_to_all(jnp.stack([bank_part] * lax.axis_size('bat...  20.1 us
  transfers between devices with their start and end apart: 3, of which 2 were waited for; matrix products, arithmetic and copies ran while one was open for 7% of the time, Pallas kernels for 0%

profile of v1, /device:TPU:1, one launch (start us, length us, event | category | flops | bytes accessed | tf_op | source)
XLA Modules:
  0.0 828.0 jit_solution(13533640267203988518)
XLA Ops:
  7.2 1.3 fusion.60
  10.9 2.2 copy.33
  13.1 15.2 %all-to-all-start.3 = ((bf16[1,9,512,128]{3,1,0,2:T(8,128)(2,1)}), bf16[1,9,512,128]{3,1,0,2:T(8,128)(2,1)S(1)}, u32[]{:S(2)}, u32[]{:S(2)}) async-start(bf16[1,9,512,128]{3,1,0,2:T(8,128)(2,1)} %copy.33), calls=%async_computation.3 | async-start | bytes 4194304 | tf_op jit(solution)/shard_map/all_to_all | solution.py:54
  28.8 0.5 fusion.76
  29.4 0.5 fusion.74
  29.9 0.5 fusion.72
  30.5 0.5 fusion.70
  31.0 0.5 fusion.68
  31.6 0.6 fusion.66
  32.1 0.5 fusion.64
  32.6 0.5 fusion.62
  33.2 2.2 copy.29
  35.4 44.3 %all-to-all-done.3 = bf16[1,9,512,128]{3,1,0,2:T(8,128)(2,1)S(1)} async-done(((bf16[1,9,512,128]{3,1,0,2:T(8,128)(2,1)}), bf16[1,9,512,128]{3,1,0,2:T(8,128)(2,1)S(1)}, u32[]{:S(2)}, u32[]{:S(2)}) %all-to-all-start.3) | async-done | bytes 1179680 | tf_op jit(solution)/shard_map/all_to_all | solution.py:54
  79.7 45.8 %all_to_all.40 = bf16[1,9,512,128]{3,1,0,2:T(8,128)(2,1)} all-to-all(bf16[1,9,512,128]{3,1,0,2:T(8,128)(2,1)} %copy.29), channel_id=1, replica_groups=mesh['batch'=64,'chan'=4] {'batch'}, dimensions={2} | all-to-all | bytes 2359296 | tf_op jit(solution)/shard_map/all_to_all | solution.py:54
  125.5 2.3 stack.55
  127.8 168.0 %all_to_all.41 = bf16[64,8,9,8,128]{4,3,2,1,0:T(8,128)(2,1)} all-to-all(bf16[64,8,9,8,128]{4,3,2,1,0:T(8,128)(2,1)S(1)} %stack.55), channel_id=1, replica_groups=mesh['batch'=64,'chan'=4] {'batch'}, dimensions={0} | all-to-all | bytes 18874368 | tf_op jit(solution)/shard_map/all_to_all | solution.py:45
  295.8 5.9 stack.44
  301.7 6.0 all-to-all-start
  307.8 0.6 copy.43
  308.4 0.6 copy.42
  309.0 0.8 pad_slice_fusion.24
  309.8 1.3 pad_slice_fusion.16
  311.5 1.4 reshape.895
  312.9 0.6 copy-done
  313.9 0.5 reshape.862
  314.4 0.6 fusion.166
  315.0 10.1 %copy.32 = bf16[8,9,64,8,128]{4,3,2,1,0:T(8,128)(2,1)} copy(bf16[8,9,64,8,128]{4,3,1,0,2:T(8,128)(2,1)} %bitcast.536) | data formatting | bytes 18874368 | tf_op jit(solution)/shard_map/reshape | solution.py:44
  325.0 16.2 %copy.60 = bf16[1,8,4608,128]{3,1,2,0:T(8,128)(2,1)S(1)} copy(bf16[1,8,4608,128]{3,2,1,0:T(8,128)(2,1)} %bitcast.537) | data formatting | bytes 18874368
  341.3 8.0 fusion.146
  349.5 157.5 %all-to-all-done = bf16[64,8,9,8,128]{4,3,2,1,0:T(8,128)(2,1)} async-done(((bf16[64,8,9,8,128]{4,3,2,1,0:T(8,128)(2,1)}), bf16[64,8,9,8,128]{4,3,2,1,0:T(8,128)(2,1)}, u32[]{:S(2)}, u32[]{:S(2)}) %all-to-all-start) | async-done | bytes 9437216 | tf_op jit(solution)/shard_map/all_to_all | solution.py:45
  507.0 10.0 %copy.27 = bf16[8,9,64,8,128]{4,3,2,1,0:T(8,128)(2,1)} copy(bf16[8,9,64,8,128]{4,3,1,0,2:T(8,128)(2,1)} %bitcast.4) | data formatting | bytes 18874368 | tf_op jit(solution)/shard_map/reshape | solution.py:44
  517.0 16.2 %copy.61 = bf16[1,8,4608,128]{3,1,2,0:T(8,128)(2,1)S(1)} copy(bf16[1,8,4608,128]{3,2,1,0:T(8,128)(2,1)} %bitcast.538) | data formatting | bytes 18874368
  533.3 8.0 fusion.148
  541.5 0.8 copy-done.12
  548.4 0.5 copy-done.5
  552.8 0.9 fusion.6
  553.7 1.9 fusion.4
  555.6 1.2 copy-done.1
  556.9 0.6 fusion.167
  557.4 0.8 copy.35
  558.2 0.8 copy.36
  560.0 254.0 %all-reduce.4 = (f32[64,8]{1,0:T(8,128)S(1)}, f32[64,8]{1,0:T(8,128)S(1)}) all-reduce(f32[64,8]{1,0:T(8,128)S(1)} %fusion.125, f32[64,8]{1,0:T(8,128)S(1)} %fusion.122), channel_id=1, replica_groups=mesh['batch'=64,'chan'=4] {'batch','chan'}, use_global_device_ids=true, to_apply=%region_1.2 | all-reduce | flops 1024 | bytes 8192 | tf_op jit(solution)/shard_map/psum | solution.py:86
  814.0 0.6 multiply_reduce_fusion
  814.7 0.6 multiply_reduce_fusion.1
  815.3 1.2 subtract_multiply_fusion
  816.4 1.2 subtract_multiply_fusion.1
  817.6 1.7 convert_convert_fusion
  819.3 1.5 convert_convert_fusion.1
  (97 shorter events, 14.9 us)
Async XLA Ops:
  7.2 1.3 copy-start.13
  7.2 1.3 copy-start.32
  13.1 15.3 %copy-start.4 = (bf16[1,32,32,128]{3,2,1,0:T(8,128)(2,1)S(1)}, bf16[1,32,32,128]{3,2,1,0:T(8,128)(2,1)}, u32[]{:S(2)}) copy-start(bf16[1,32,32,128]{3,2,1,0:T(8,128)(2,1)} %param.9) | copy-start | bytes 786436
  13.1 15.3 %copy-start.31 = (bf16[1,32,32,512]{3,2,1,0:T(8,128)(2,1)S(1)}, bf16[1,32,32,512]{3,2,1,0:T(8,128)(2,1)}, u32[]{:S(2)}) copy-start(bf16[1,32,32,512]{3,2,1,0:T(8,128)(2,1)} %param.8) | copy-start | bytes 3145732
  13.1 66.6 %all-to-all-start.3 = ((bf16[1,9,512,128]{3,1,0,2:T(8,128)(2,1)}), bf16[1,9,512,128]{3,1,0,2:T(8,128)(2,1)S(1)}, u32[]{:S(2)}, u32[]{:S(2)}) async-start(bf16[1,9,512,128]{3,1,0,2:T(8,128)(2,1)} %copy.33), calls=%async_computation.3 | async-start | bytes 4194304 | tf_op jit(solution)/shard_map/all_to_all | solution.py:54
  35.4 90.1 %copy-start.23 = (bf16[8,9,8,128]{3,2,1,0:T(8,128)(2,1)S(1)}, bf16[8,9,8,128]{3,2,1,0:T(8,128)(2,1)}, u32[]{:S(2)}) copy-start(bf16[8,9,8,128]{3,2,1,0:T(8,128)(2,1)} %param.14) | copy-start | bytes 442372
  127.8 168.0 %copy-start.25 = (bf16[8,9,8,128]{3,2,1,0:T(8,128)(2,1)S(1)}, bf16[8,9,8,128]{3,2,1,0:T(8,128)(2,1)}, u32[]{:S(2)}) copy-start(bf16[8,9,8,128]{3,2,1,0:T(8,128)(2,1)} %param.10) | copy-start | bytes 442372
  301.7 6.0 copy-start.27
  301.7 6.0 copy-start.28
  301.7 205.3 %all-to-all-start = ((bf16[64,8,9,8,128]{4,3,2,1,0:T(8,128)(2,1)}), bf16[64,8,9,8,128]{4,3,2,1,0:T(8,128)(2,1)}, u32[]{:S(2)}, u32[]{:S(2)}) async-start(bf16[64,8,9,8,128]{4,3,2,1,0:T(8,128)(2,1)} %stack.44), calls=%async_computation | async-start | bytes 18874368 | tf_op jit(solution)/shard_map/all_to_all | solution.py:45
  307.7 509.9 %all-reduce.8.cloned.1.call-start = ((), (), s32[]{:S(2)}) async-start(), calls=%async_computation.4 | async-start | bytes 2621440 | tf_op jit(solution)/shard_map/psum | solution.py:51
  311.5 2.0 copy-start
  314.4 10.6 %copy-start.2 = (bf16[64,9216]{1,0:T(8,128)(2,1)}, bf16[64,9216]{1,0:T(8,128)(2,1)S(1)}, u32[]{:S(2)}) copy-start(bf16[64,9216]{1,0:T(8,128)(2,1)S(1)} %reshape.862) | copy-start | bytes 3538948
  541.3 1.0 copy-start.12
  542.2 0.9 copy-start.11
  543.2 0.9 copy-start.10
  544.1 0.9 copy-start.9
  545.1 0.9 copy-start.8
  546.0 0.9 copy-start.7
  547.0 0.9 copy-start.6
  547.9 0.9 copy-start.5
  548.9 0.8 copy-start.21
  548.9 1.1 copy-start.20
  549.3 0.9 copy-start.19
  550.0 0.8 copy-start.18
  550.2 0.8 copy-start.14
  550.8 0.8 copy-start.17
  551.1 0.8 copy-start.16
  551.7 0.8 copy-start.15
  551.9 0.8 copy-start.22
  555.6 1.3 copy-start.1
  556.9 2.1 copy-start.24
  558.2 1.4 copy-start.3
  558.2 1.4 copy-start.26
  559.4 254.6 %copy-start.30 = (f32[1,8]{1,0:T(1,128)S(1)}, f32[1,8]{1,0:T(1,128)}, u32[]{:S(2)}) copy-start(f32[1,8]{1,0:T(1,128)} %copy.43) | copy-start | bytes 100
  559.4 255.2 %copy-start.29 = (f32[1,8]{1,0:T(1,128)S(1)}, f32[1,8]{1,0:T(1,128)}, u32[]{:S(2)}) copy-start(f32[1,8]{1,0:T(1,128)} %copy.42) | copy-start | bytes 100
Sparse Core Ops, SparseCore 0:
  555.7 227.9 all-reduce.7
